TPU v7x, 128 devices: a whole 4x4x4 slice. The times are simulated.
128 devices in a mesh: batch: 2 (over core), sx: 8 (over y, x_lo), sy: 8 (over x_hi, z).
Axes of the slice: x: 4 (x_hi: 2, x_lo: 2; x = x_hi * 2 + x_lo), y: 4, z: 4, core: 2. Of those that a mesh axis runs over, the one named last changes fastest.
Arguments:
- features: bfloat16 [2, 32, 32, 64, 128], P('batch', None, 'sx', 'sy'), may hold values from -6 to 6
- labels: int32 [2, 32, 64, 128], P('batch', 'sx', 'sy'), may hold values from 0 to 3
- w_enc: bfloat16 [3, 3, 3, 32, 32], replicated, may hold values from -0.21875 to 0.21875
- w_mid: bfloat16 [3, 3, 3, 64, 32], replicated, may hold values from -0.21875 to 0.21875
- w_dec: bfloat16 [3, 3, 3, 32, 96], replicated, may hold values from -0.125 to 0.125
- w_out: bfloat16 [4, 32], replicated, may hold values from -1 to 1
Outputs:
- feature_grad: bfloat16 [2, 32, 32, 64, 128], P('batch', None, 'sx', 'sy')
- grad_enc: float32 [3, 3, 3, 32, 32], replicated
- grad_mid: float32 [3, 3, 3, 64, 32], replicated
- grad_dec: float32 [3, 3, 3, 32, 96], replicated
- grad_out: float32 [4, 32], replicated
All inputs are finite; a program needn't handle non-finite values.
Results may differ from a plain program's by a relative error of at most 0.012.
Values may be sent and summed in bfloat16 or wider, within the bound.
A program may use at most 128 MiB of HBM per device.

v0:
```python
import functools

import jax
import jax.numpy as jnp
from jax import lax
from jax.experimental import pallas as pl
from jax.experimental.pallas import tpu as pltpu
from jax.sharding import PartitionSpec as P

loss_scale = 32.0
LANES = 128
MESH = pl.DeviceIdType.MESH
f32 = jnp.float32
bf16 = jnp.bfloat16

DIRS = [(0, -1), (0, 1), (-1, -1), (-1, 1), (1, -1), (1, 1), (-1, 0), (1, 0)]
FEAT, POOL, SKIP, MID, DECG, MIDG, ENCG = range(7)
DEC, MIDW, ENC = range(3)


def lane_tile(y, count=1):
    if isinstance(y, int):
        return pl.ds(y * LANES, count * LANES)
    return pl.ds(pl.multiple_of(y * LANES, LANES), count * LANES)


def sigmoid(u):
    return 1.0 / (1.0 + jnp.exp(-u))


def shifted(tile, shift):
    lane = lax.broadcasted_iota(jnp.int32, tile.shape, 1)
    before = jnp.where(lane >= shift, pltpu.roll(tile, shift, axis=1), 0.0)
    after = jnp.where(lane < LANES - shift, pltpu.roll(tile, LANES - shift, axis=1), 0.0)
    return before.astype(bf16), after.astype(bf16)


def pair_sum(tile):
    lane = lax.broadcasted_iota(jnp.int32, tile.shape, 1)
    other = jnp.where(
        lane % 2 == 0, pltpu.roll(tile, LANES - 1, axis=1), pltpu.roll(tile, 1, axis=1)
    )
    return tile + other


def packed(tile):
    half = tile.shape[0] // 2
    lane = lax.broadcasted_iota(jnp.int32, (half, LANES), 1)
    return jnp.where(lane % 2 == 0, tile[:half], tile[half:]).astype(bf16)


def unpacked(tile):
    tile = tile.astype(f32)
    lane = lax.broadcasted_iota(jnp.int32, tile.shape, 1)
    first = jnp.where(lane % 2 == 0, tile, pltpu.roll(tile, 1, axis=1))
    second = jnp.where(lane % 2 == 1, tile, pltpu.roll(tile, LANES - 1, axis=1))
    return jnp.concatenate([first, second], axis=0)


def put_sides(buf, x, y, tile, period, offset, shift, back):
    chans = tile.shape[0]
    before, after = shifted(tile, shift)
    lanes = lane_tile(y)
    buf[x, offset : offset + chans, lanes] = after if back else before
    buf[x, 2 * period + offset : 2 * period + offset + chans, lanes] = before if back else after


def put_stack(buf, x, y, tile, period, offset, shift, back=False):
    chans = tile.shape[0]
    buf[x, period + offset : period + offset + chans, lane_tile(y)] = tile.astype(bf16)
    put_sides(buf, x, y, tile, period, offset, shift, back)


def each(first, last, step, carry):
    for at in range(first, last):
        step(at, carry)


def over_halo(nx, ny, step):
    for x in range(nx + 2):
        for y in range(ny + 2):
            if x in (0, nx + 1) or y in (0, ny + 1):
                step(x, y)


def finish_halo(buf, nx, ny, chans, period, offset, shift, back=False):
    def step(x, y):
        tile = buf[x, period + offset : period + offset + chans, lane_tile(y)].astype(f32)
        put_sides(buf, x, y, tile, period, offset, shift, back)

    over_halo(nx, ny, step)


def finish_inner(buf, nx, ny, chans, shift, back=False):
    for x in range(1, nx + 1):
        for y in range(1, ny + 1):
            tile = buf[x, chans : 2 * chans, lane_tile(y)].astype(f32)
            put_sides(buf, x, y, tile, chans, 0, shift, back)


def unpack_halo(buf, landed, nx, ny, chans, back=False):
    def step(x, y):
        put_stack(buf, x, y, unpacked(landed[x, :, lane_tile(y)]), chans, 0, 2, back)

    over_halo(nx, ny, step)


def clear_halo(buf, nx, ny, low, high):
    width = (ny + 2) * LANES
    buf[0, low:high, :] = jnp.zeros((high - low, width), bf16)
    buf[nx + 1, low:high, :] = jnp.zeros((high - low, width), bf16)
    for x in range(1, nx + 1):
        buf[x, low:high, lane_tile(0)] = jnp.zeros((high - low, LANES), bf16)
        buf[x, low:high, lane_tile(ny + 1)] = jnp.zeros((high - low, LANES), bf16)


def taps(fields, x, y, count, low, high, back=False):
    depth = sum(rows for _, _, rows in fields)
    parts = []
    for window in range(9):
        a, b = divmod(8 - window if back else window, 3)
        start = window * depth
        for buf, base, rows in fields:
            first, last = max(low, start), min(high, start + rows)
            if first < last:
                where = slice(base + first - start, base + last - start)
                parts.append(buf[x + a, where, lane_tile(y + b, count)])
            start += rows
    return parts[0] if len(parts) == 1 else jnp.concatenate(parts, axis=0)


def conv(weight, buf, x, tiles, back=False):
    depth = buf.shape[1]
    fields = [(buf, 0, depth)]
    y, other = tiles
    if other == y + 1:
        window = taps(fields, x, y, 2, 0, 9 * depth, back)
    else:
        window = jnp.concatenate(
            [taps(fields, x, at, 1, 0, 9 * depth, back) for at in tiles], axis=1
        )
    return jnp.dot(weight[...], window, preferred_element_type=f32)


def inner_pairs(ny):
    return [(y, y + 1) for y in range(1, ny - 1, 2)]


def all_pairs(ny):
    return [(y, y + 1) for y in range(0, ny, 2)]


def ranges_of(nx):
    return [(1, 3) if x == 0 else (0, 2) if x == nx - 1 else (0, 3) for x in range(nx)]


def local_part(sums, weights, buf, nx, ny, first):
    for x, (low, high) in enumerate(ranges_of(nx)):
        for y in range(1, ny + 1, 2):
            lanes = lane_tile(y, 2)
            window = jnp.concatenate([buf[x + a, :, lanes] for a in range(low, high)], axis=0)
            term = jnp.dot(weights[low, high][...], window, preferred_element_type=f32)
            if first:
                sums[x, :, lanes] = term
            else:
                sums[x, :, lanes] += term


def border_part(sums, weights, buf, nx, ny, first):
    sides = (lane_tile(0), lane_tile(ny + 1))
    for x in range(nx):
        window = jnp.concatenate(
            [jnp.concatenate([buf[x + a, :, s] for s in sides], axis=1) for a in range(3)], axis=0
        )
        term = jnp.dot(weights[0, 3][...], window, preferred_element_type=f32)
        for at, lanes in enumerate(sides):
            part = term[:, at * LANES : (at + 1) * LANES]
            if first:
                sums[x, :, lanes] = part
            else:
                sums[x, :, lanes] += part
    for x, a in ((0, 0), (nx - 1, 2)):
        for y in range(1, ny + 1, 2):
            lanes = lane_tile(y, 2)
            sums[x, :, lanes] += jnp.dot(
                weights[a, a + 1][...], buf[x + a, :, lanes], preferred_element_type=f32
            )


def weight_grad(total, grads, fields, size_x, count):
    width = 9 * sum(rows for _, _, rows in fields)
    for low in range(0, width, 256):
        high = min(low + 256, width)
        acc = None
        for x in range(size_x):
            term = lax.dot_general(
                grads(x),
                taps(fields, x, 0, count, low, high),
                (((1,), (1,)), ((), ())),
                preferred_element_type=f32,
            )
            acc = term if acc is None else acc + term
        total[:, low:high] = acc
    rest = total.shape[1] - width
    total[:, width:] = jnp.zeros((total.shape[0], rest), f32)


def laid_lanes(w, order):
    return jnp.concatenate([w[t] for t in order], axis=1)


def forward_weights(dest, w):
    for low in range(0, 27, 4):
        high = min(low + 4, 27)
        dest[:, low * 32 : high * 32] = laid_lanes(w, range(low, high))


def window_weights(dests, w, first, last):
    for (low, high), dest in dests.items():
        for b in range(3):
            parts = [
                w[(a * 3 + b) * 3 + c, :, first:last] for a in range(low, high) for c in range(3)
            ]
            dest[b * 32 : (b + 1) * 32, :] = jnp.concatenate(parts, axis=1)


def turned_weights(dest, w):
    count, outs, ins = w.shape
    flat = w[...].astype(f32).reshape(count * outs, ins)
    dest[...] = flat.T.astype(bf16)


def kernel(
    sizes,
    feat_hbm,
    labels_hbm,
    w_enc_hbm,
    w_mid_hbm,
    w_dec_hbm,
    w_out_hbm,
    feature_grad_hbm,
    sum_dec,
    sum_mid,
    sum_enc,
    feat,
    labels,
    w_enc,
    w_mid,
    w_dec,
    w_out,
    load_sem,
    feature_grad,
    store_sem,
    w_enc_f,
    w_enc_b,
    w_mid_f,
    w_mid_b,
    w_skip_03,
    w_skip_13,
    w_skip_02,
    w_skip_01,
    w_skip_23,
    w_up_03,
    w_up_13,
    w_up_02,
    w_up_01,
    w_up_23,
    w_dec_b,
    rows32,
    window_sums,
    F,
    PO,
    PP,
    UP,
    JU,
    JE,
    D,
    MG,
    MGP,
    EG,
    enc_slope,
    mid_slope,
    joined_grad,
    out_total,
    total_dec,
    total_mid,
    total_enc,
    part_dec,
    part_mid,
    part_enc,
    rs_dec,
    rs_mid,
    rs_enc,
    ar_dec,
    ar_mid,
    ar_enc,
    ag_dec,
    ag_mid,
    ag_enc,
    halo_send,
    halo_recv,
    rs_send,
    rs_recv,
    ar_send,
    ar_recv,
    ag_send,
    ag_recv,
):
    nb, nsx, nsy, nx, ny = sizes
    cx, cy = nx // 2, ny // 2
    half = nsy // 2
    near, far = nb * half, nsx * 2
    bt, sx, sy = lax.axis_index("batch"), lax.axis_index("sx"), lax.axis_index("sy")
    here, there = bt * half + lax.rem(sy, half), sx * 2 + sy // half
    skip_weights = {
        (0, 3): w_skip_03,
        (1, 3): w_skip_13,
        (0, 2): w_skip_02,
        (0, 1): w_skip_01,
        (2, 3): w_skip_23,
    }
    up_weights = {
        (0, 3): w_up_03,
        (1, 3): w_up_13,
        (0, 2): w_up_02,
        (0, 1): w_up_01,
        (2, 3): w_up_23,
    }

    loads = {
        name: pltpu.make_async_copy(source, dest, load_sem.at[at])
        for at, (name, source, dest) in enumerate(
            (
                ("feat", feat_hbm, feat),
                ("w_enc", w_enc_hbm, w_enc),
                ("w_mid", w_mid_hbm, w_mid),
                ("w_dec", w_dec_hbm, w_dec),
                ("w_out", w_out_hbm, w_out),
                ("labels", labels_hbm, labels),
            )
        )
    }
    for load in loads.values():
        load.start()

    clear_halo(F, nx, ny, 32, 64)
    clear_halo(PP, cx, cy, 0, 16)
    clear_halo(JE, nx, ny, 32, 64)
    clear_halo(UP, cx, cy, 0, 32)
    clear_halo(D, nx, ny, 32, 64)
    clear_halo(MGP, cx, cy, 0, 32)
    clear_halo(EG, nx, ny, 32, 64)

    def near_peer(k):
        return lax.rem(here + k, near)

    def near_id(p):
        return (p // half, sx, (sy // half) * half + lax.rem(p, half))

    def far_peer(k):
        return lax.rem(there + k, far)

    def far_id(q):
        return (bt, q // 2, lax.rem(q, 2) * half + lax.rem(sy, half))

    barrier = pltpu.get_barrier_semaphore()
    for dx, dy in DIRS:
        pl.semaphore_signal(
            barrier,
            inc=1,
            device_id=(bt, lax.rem(sx + dx + nsx, nsx), lax.rem(sy + dy + nsy, nsy)),
            device_id_type=MESH,
        )
    for k in range(1, far):
        pl.semaphore_signal(barrier, inc=1, device_id=far_id(far_peer(k)), device_id_type=MESH)
    for k in range(1, near):
        pl.semaphore_signal(barrier, inc=1, device_id=near_id(near_peer(k)), device_id_type=MESH)

    loads["feat"].wait()

    def load_features(x, carry):
        rows32[x] = feat[:, x].astype(f32).reshape(32 * ny, LANES)
        for y in range(ny):
            put_stack(F, x + 1, y + 1, rows32[x, pl.ds(y, 32, stride=ny), :], 32, 0, 1)
        return carry

    each(0, nx, load_features, 0)

    pl.semaphore_wait(barrier, near - 1 + far - 1 + 8)

    fields = {
        FEAT: (F, nx, ny, 32, 64),
        POOL: (PP, cx, cy, 0, 16),
        SKIP: (JE, nx, ny, 32, 64),
        MID: (UP, cx, cy, 0, 32),
        DECG: (D, nx, ny, 32, 64),
        MIDG: (MGP, cx, cy, 0, 32),
        ENCG: (EG, nx, ny, 32, 64),
    }

    def halo_copy(field, index):
        buf, sizex, sizey, low, high = fields[field]
        dx, dy = DIRS[index]

        def source(step, size):
            return {-1: (1, 1), 0: (1, size), 1: (size, 1)}[step]

        def target(step, size):
            return {-1: (size + 1, 1), 0: (1, size), 1: (0, 1)}[step]

        (x0, xn), (y0, yn) = source(dx, sizex), source(dy, sizey)
        (tx0, _), (ty0, _) = target(dx, sizex), target(dy, sizey)
        return pltpu.make_async_remote_copy(
            src_ref=buf.at[pl.ds(x0, xn), low:high, lane_tile(y0, yn)],
            dst_ref=buf.at[pl.ds(tx0, xn), low:high, lane_tile(ty0, yn)],
            send_sem=halo_send.at[field, index],
            recv_sem=halo_recv.at[field, index],
            device_id=(bt, lax.rem(sx + dx + nsx, nsx), lax.rem(sy + dy + nsy, nsy)),
            device_id_type=MESH,
        )

    def inside(dx, dy):
        ok = None
        for step, at, size in ((dx, sx, nsx), (dy, sy, nsy)):
            if step:
                this = at > 0 if step < 0 else at < size - 1
                ok = this if ok is None else jnp.logical_and(ok, this)
        return ok

    def start_halo(field):
        for index, (dx, dy) in enumerate(DIRS):

            @pl.when(inside(dx, dy))
            def _():
                halo_copy(field, index).start()

    def wait_halo(field):
        for index, (dx, dy) in enumerate(DIRS):

            @pl.when(inside(-dx, -dy))
            def _():
                halo_copy(field, index).wait_recv()

    def wait_halo_sent(field):
        for index, (dx, dy) in enumerate(DIRS):

            @pl.when(inside(dx, dy))
            def _():
                halo_copy(field, index).wait_send()

    cut_dec = [(0, 96, 128 * j, 128) for j in range(8)]
    cut_mid = [(0, 64, 128 * j, 128) for j in range(8)]
    cut_enc = [(48 * (j % 2), 48, 128 * (j // 2), 128) for j in range(6)] + [None] * 2
    sums = {
        DEC: (total_dec, part_dec, rs_dec, ar_dec, ag_dec, cut_dec),
        MIDW: (total_mid, part_mid, rs_mid, ar_mid, ag_mid, cut_mid),
        ENC: (total_enc, part_enc, rs_enc, ar_enc, ag_enc, cut_enc),
    }

    def rs_copy(g, k):
        _, part, landing, _, _, _ = sums[g]
        return pltpu.make_async_remote_copy(
            src_ref=part.at[near_peer(k)],
            dst_ref=landing.at[here],
            send_sem=rs_send.at[g],
            recv_sem=rs_recv.at[g],
            device_id=near_id(near_peer(k)),
            device_id_type=MESH,
        )

    def ar_copy(g, k):
        landing = sums[g][3]
        return pltpu.make_async_remote_copy(
            src_ref=landing.at[there],
            dst_ref=landing.at[there],
            send_sem=ar_send.at[g],
            recv_sem=ar_recv.at[g],
            device_id=far_id(far_peer(k)),
            device_id_type=MESH,
        )

    def ag_copy(g, k):
        landing = sums[g][4]
        return pltpu.make_async_remote_copy(
            src_ref=landing.at[here],
            dst_ref=landing.at[here],
            send_sem=ag_send.at[g],
            recv_sem=ag_recv.at[g],
            device_id=near_id(near_peer(k)),
            device_id_type=MESH,
        )

    def wait_bytes(sem, pieces):
        pltpu.make_async_copy(pieces, pieces, sem).wait()

    def start_scatter(g):
        total, part, _, _, _, cut = sums[g]
        for j in range(near):
            if cut[j] is None:
                part[j] = jnp.zeros(part.shape[1:], bf16)
            else:
                row, rows, lane, lanes = cut[j]
                part[j] = total[row : row + rows, lane : lane + lanes].astype(bf16)
        for k in range(1, near):
            rs_copy(g, k).start()

    def start_exchange(g):
        _, part, landing, mine, _, _ = sums[g]
        wait_bytes(rs_recv.at[g], landing.at[pl.ds(0, near - 1)])
        acc = part[here].astype(f32)
        for k in range(1, near):
            acc = acc + landing[near_peer(k)].astype(f32)
        mine[there] = acc.astype(bf16)
        for k in range(1, far):
            ar_copy(g, k).start()

    def start_gather(g):
        _, _, _, landing, result, _ = sums[g]
        wait_bytes(ar_recv.at[g], landing.at[pl.ds(0, far - 1)])
        acc = landing[0].astype(f32)
        for q in range(1, far):
            acc = acc + landing[q].astype(f32)
        result[here] = acc.astype(bf16)
        for k in range(1, near):
            ag_copy(g, k).start()

    def wait_gather(g):
        wait_bytes(ag_recv.at[g], sums[g][4].at[pl.ds(0, near - 1)])

    def wait_scatter_sent(g):
        wait_bytes(rs_send.at[g], sums[g][1].at[pl.ds(0, near - 1)])

    def wait_exchange_sent(g):
        wait_bytes(ar_send.at[g], sums[g][3].at[pl.ds(0, far - 1)])

    def wait_gather_sent(g):
        wait_bytes(ag_send.at[g], sums[g][4].at[pl.ds(0, near - 1)])

    start_halo(FEAT)
    for name in ("w_enc", "w_mid", "w_dec", "w_out", "labels"):
        loads[name].wait()
    forward_weights(w_enc_f, w_enc)

    def enc_tiles(x, tiles):
        pre = conv(w_enc_f, F, x, tiles)
        s = sigmoid(pre)
        slope = s * (1.0 + pre * (1.0 - s))
        act = (pre * s).astype(bf16).astype(f32)
        for at, y in enumerate(tiles):
            lanes = slice(at * LANES, (at + 1) * LANES)
            enc_slope[x, :, lane_tile(y)] = slope[:, lanes]
            JE[x + 1, 32:64, lane_tile(y + 1)] = act[:, lanes].astype(bf16)

    def enc_inner(x, carry):
        for tiles in inner_pairs(ny):
            enc_tiles(x, tiles)
        return carry

    each(1, nx - 1, enc_inner, 0)
    turned_weights(w_mid_f, w_mid)
    window_weights(skip_weights, w_dec, 64, 96)
    window_weights(up_weights, w_dec, 0, 64)
    out_total[...] = jnp.zeros(out_total.shape, f32)
    wait_halo(FEAT)
    finish_halo(F, nx, ny, 32, 32, 0, 1)

    def enc_sides(x, carry):
        enc_tiles(x, (0, ny - 1))
        return carry

    each(1, nx - 1, enc_sides, 0)

    def enc_ends(i, carry):
        for tiles in all_pairs(ny):
            enc_tiles(i * (nx - 1), tiles)
        return carry

    each(0, 2, enc_ends, 0)

    def pool_block(bx, carry):
        for by in range(cy):
            block = jnp.zeros((32, LANES), f32)
            for dx in range(2):
                for dy in range(2):
                    block += JE[2 * bx + dx + 1, 32:64, lane_tile(2 * by + dy + 1)].astype(f32)
            pooled = (pair_sum(block) * 0.125).astype(bf16).astype(f32)
            PP[bx + 1, :, lane_tile(by + 1)] = packed(pooled)
            PO[bx + 1, 32:64, lane_tile(by + 1)] = pooled.astype(bf16)
        return carry

    each(0, cx, pool_block, 0)
    start_halo(POOL)
    start_halo(SKIP)
    finish_inner(PO, cx, cy, 32, 2)
    finish_inner(JE, nx, ny, 32, 1)
    local_part(window_sums, skip_weights, JE, nx, ny, True)
    turned_weights(w_enc_b, w_enc)
    turned_weights(w_dec_b, w_dec)
    for low in range(0, 27, 2):
        high = min(low + 2, 27)
        w_mid_b[:, low * 64 : high * 64] = laid_lanes(w_mid, range(low, high))
    wait_halo(POOL)
    unpack_halo(PO, PP, cx, cy, 32)

    def mid_block(bx, carry):
        for by in range(0, cy, 2):
            pre = conv(w_mid_f, PO, bx, (by, by + 1))
            s = sigmoid(pre)
            mid_slope[bx, :, lane_tile(by, 2)] = s * (1.0 + pre * (1.0 - s))
            act = (pre * s).astype(bf16)
            for dy in range(2):
                tile = act[:, dy * LANES : (dy + 1) * LANES]
                UP[bx + 1, :, lane_tile(by + dy + 1)] = packed(tile.astype(f32))
                JU[2 * bx + 1, 64:128, lane_tile(2 * (by + dy) + 1)] = tile
        return carry

    each(0, cx, mid_block, 0)
    start_halo(MID)

    def spread(bx, by, tile):
        before, after = shifted(tile, 1)
        tile = tile.astype(bf16)
        for x in (2 * bx - 1, 2 * bx):
            for y in (2 * by - 1, 2 * by):
                if 0 <= x <= nx + 1 and 0 <= y <= ny + 1:
                    lanes = lane_tile(y)
                    JU[x, 0:64, lanes] = before
                    JU[x, 64:128, lanes] = tile
                    JU[x, 128:192, lanes] = after

    for bx in range(1, cx + 1):
        for by in range(1, cy + 1):
            spread(bx, by, JU[2 * bx - 1, 64:128, lane_tile(2 * by - 1)].astype(f32))
    local_part(window_sums, up_weights, JU, nx, ny, False)
    wait_halo(SKIP)
    finish_halo(JE, nx, ny, 32, 32, 0, 1)
    border_part(window_sums, skip_weights, JE, nx, ny, True)
    wait_halo(MID)
    for bx in range(cx + 2):
        for by in range(cy + 2):
            if bx in (0, cx + 1) or by in (0, cy + 1):
                spread(bx, by, unpacked(UP[bx, :, lane_tile(by)]))

    border_part(window_sums, up_weights, JU, nx, ny, False)

    def dec_row(x, carry):
        pre = (
            window_sums[x, 0:32, lane_tile(0, ny)]
            + window_sums[x, 32:64, lane_tile(1, ny)]
            + window_sums[x, 64:96, lane_tile(2, ny)]
        )
        s = sigmoid(pre)
        slope = s * (1.0 + pre * (1.0 - s))
        act = (pre * s).astype(bf16)
        logits = jnp.dot(w_out[...], act, preferred_element_type=f32)
        expo = jnp.exp(logits)
        prob = expo / jnp.sum(expo, axis=0, keepdims=True)
        ids = lax.broadcasted_iota(jnp.int32, prob.shape, 0)
        these = jnp.concatenate([labels[x, y : y + 1, :] for y in range(ny)], axis=1)
        onehot = (these == ids).astype(f32)
        logit_grad = (loss_scale * (prob - onehot)).astype(bf16)
        out_total[...] += lax.dot_general(
            logit_grad, act, (((1,), (1,)), ((), ())), preferred_element_type=f32
        )
        act_grad = lax.dot_general(
            w_out[...], logit_grad, (((0,), (0,)), ((), ())), preferred_element_type=f32
        )
        grads = (act_grad * slope).astype(bf16).astype(f32)
        for y in range(ny):
            tile = grads[:, y * LANES : (y + 1) * LANES]
            D[x + 1, 32:64, lane_tile(y + 1)] = tile.astype(bf16)
        return carry

    each(0, nx, dec_row, 0)
    start_halo(DECG)
    finish_inner(D, nx, ny, 32, 1, back=True)

    def dec_back(x, tiles):
        grads = conv(w_dec_b, D, x, tiles, back=True)
        for at, y in enumerate(tiles):
            joined_grad[x, :, lane_tile(y)] = grads[:, at * LANES : (at + 1) * LANES]

    def dec_back_inner(x, carry):
        for tiles in inner_pairs(ny):
            dec_back(x, tiles)
        return carry

    each(1, nx - 1, dec_back_inner, 0)
    joined = [(JU, 64, 64), (JE, 32, 32)]
    weight_grad(total_dec, lambda x: D[x + 1, :, lane_tile(1, ny)], joined, nx, ny)
    total_dec[0:4, 864:896] = out_total[...]
    start_scatter(DEC)

    wait_halo(DECG)
    finish_halo(D, nx, ny, 32, 32, 0, 1, back=True)

    def dec_back_sides(x, carry):
        dec_back(x, (0, ny - 1))
        return carry

    each(1, nx - 1, dec_back_sides, 0)

    def dec_back_ends(i, carry):
        for tiles in all_pairs(ny):
            dec_back(i * (nx - 1), tiles)
        return carry

    each(0, 2, dec_back_ends, 0)

    def mid_grads(bx, carry):
        for by in range(cy):
            block = jnp.zeros((64, LANES), f32)
            for dx in range(2):
                for dy in range(2):
                    block += joined_grad[2 * bx + dx, 0:64, lane_tile(2 * by + dy)]
            grads = pair_sum(block) * mid_slope[bx, :, lane_tile(by)]
            grads = grads.astype(bf16).astype(f32)
            MGP[bx + 1, :, lane_tile(by + 1)] = packed(grads)
            MG[bx + 1, 64:128, lane_tile(by + 1)] = grads.astype(bf16)
        return carry

    each(0, cx, mid_grads, 0)
    start_halo(MIDG)
    finish_inner(MG, cx, cy, 64, 2, back=True)

    weight_grad(total_mid, lambda x: MG[x + 1, 64:128, lane_tile(1, cy)], [(PO, 0, 96)], cx, cy)
    start_scatter(MIDW)
    start_exchange(DEC)

    wait_halo(MIDG)
    start_exchange(MIDW)
    unpack_halo(MG, MGP, cx, cy, 64, back=True)

    def mid_back(bx, carry):
        for by in range(0, cy, 2):
            pooled = conv(w_mid_b, MG, bx, (by, by + 1), back=True) * 0.125
            for dx in range(2):
                x = 2 * bx + dx
                for dy in range(4):
                    y = 2 * by + dy
                    up = pooled[:, (dy // 2) * LANES : (dy // 2 + 1) * LANES]
                    tile = (joined_grad[x, 64:96, lane_tile(y)] + up) * enc_slope[x, :, lane_tile(y)]
                    put_stack(EG, x + 1, y + 1, tile, 32, 0, 1, back=True)
        return carry

    each(0, cx, mid_back, 0)
    start_halo(ENCG)

    weight_grad(total_enc, lambda x: EG[x + 1, :, lane_tile(1, ny)], [(F, 32, 32)], nx, ny)
    start_scatter(ENC)

    def enc_back(x, tiles):
        grads = conv(w_enc_b, EG, x, tiles, back=True)
        for at, y in enumerate(tiles):
            rows32[x, pl.ds(y, 32, stride=ny), :] = grads[:, at * LANES : (at + 1) * LANES]

    def enc_back_inner(x, carry):
        for tiles in inner_pairs(ny):
            enc_back(x, tiles)
        return carry

    each(1, nx - 1, enc_back_inner, 0)
    start_exchange(ENC)
    wait_halo(ENCG)
    finish_halo(EG, nx, ny, 32, 32, 0, 1, back=True)

    def enc_back_sides(x, carry):
        enc_back(x, (0, ny - 1))
        return carry

    each(1, nx - 1, enc_back_sides, 0)

    def enc_back_ends(i, carry):
        for tiles in all_pairs(ny):
            enc_back(i * (nx - 1), tiles)
        return carry

    each(0, 2, enc_back_ends, 0)

    def lay_out(x, carry):
        feature_grad[:, x] = rows32[x].reshape(32, ny, LANES).astype(bf16)
        return carry

    each(0, nx, lay_out, 0)
    stores = [
        pltpu.make_async_copy(source, dest, store_sem.at[at])
        for at, (source, dest) in enumerate(
            (
                (feature_grad, feature_grad_hbm),
                (ag_dec, sum_dec),
                (ag_mid, sum_mid),
                (ag_enc, sum_enc),
            )
        )
    ]
    stores[0].start()
    start_gather(DEC)
    start_gather(MIDW)
    for field in range(7):
        wait_halo_sent(field)
    for g in (DEC, MIDW, ENC):
        wait_scatter_sent(g)
    start_gather(ENC)
    wait_gather(DEC)
    stores[1].start()
    wait_gather(MIDW)
    stores[2].start()
    for g in (DEC, MIDW, ENC):
        wait_exchange_sent(g)
    for g in (DEC, MIDW):
        wait_gather_sent(g)
    wait_gather(ENC)
    stores[3].start()
    wait_gather_sent(ENC)
    for store in stores:
        store.wait()


def outputs(
    scale,
    features_in,
    dec_in,
    mid_in,
    enc_in,
    features_out,
    enc_out,
    mid_out,
    dec_out,
    out_out,
    features,
    sum_dec,
    sum_mid,
    sum_enc,
    grad_enc,
    grad_mid,
    grad_dec,
    grad_out,
    sems,
):
    copies = [
        pltpu.make_async_copy(source, dest, sems.at[at])
        for at, (source, dest) in enumerate(
            (
                (dec_in, sum_dec),
                (mid_in, sum_mid),
                (enc_in, sum_enc),
                (features_in, features),
                (grad_dec, dec_out),
                (grad_out, out_out),
                (grad_mid, mid_out),
                (grad_enc, enc_out),
                (features, features_out),
            )
        )
    ]
    for copy in copies[:4]:
        copy.start()
    copies[0].wait()
    whole = jnp.concatenate([sum_dec[j].astype(f32) for j in range(8)], axis=1) * scale
    for t in range(27):
        window, c = divmod(t, 3)
        grad_dec[t] = whole[c * 32 : (c + 1) * 32, window * 96 : (window + 1) * 96]
    grad_out[...] = whole[0:4, 864:896]
    copies[4].start()
    copies[5].start()
    copies[3].wait()
    copies[8].start()
    copies[1].wait()
    for j in range(7):
        turned = (sum_mid[j].astype(f32) * (0.5 * scale)).T
        for t in range(4 * j, min(4 * j + 4, 27)):
            grad_mid[t] = turned[(t % 4) * 32 : (t % 4 + 1) * 32]
    copies[6].start()
    copies[2].wait()
    for window in range(9):
        j, at = divmod(window, 4)
        both = jnp.concatenate([sum_enc[2 * j], sum_enc[2 * j + 1]], axis=0)
        part = both[:, at * 32 : (at + 1) * 32].astype(f32) * scale
        for c in range(3):
            grad_enc[window * 3 + c] = part[c * 32 : (c + 1) * 32]
    copies[7].start()
    for copy in copies[4:]:
        copy.wait()


def shards(features, labels, w_enc, w_mid, w_dec, w_out):
    nb, nsx, nsy = lax.axis_size("batch"), lax.axis_size("sx"), lax.axis_size("sy")
    _, chans, nx, ny, nz = features.shape
    cx, cy = nx // 2, ny // 2
    scale = 1.0 / float(nb * nsx * nsy * nx * ny * nz)
    near, far = nb * (nsy // 2), nsx * 2

    def fine(depth):
        return pltpu.VMEM((nx + 2, depth, (ny + 2) * LANES), bf16)

    def coarse(depth):
        return pltpu.VMEM((cx + 2, depth, (cy + 2) * LANES), bf16)

    pieces = ((96, 128), (64, 128), (48, 128))
    scratch = [
        pltpu.VMEM((chans, nx, ny, nz), bf16),
        pltpu.VMEM((nx, ny, nz), jnp.int32),
        pltpu.VMEM((27, 32, 32), bf16),
        pltpu.VMEM((27, 32, 64), bf16),
        pltpu.VMEM((27, 32, 96), bf16),
        pltpu.VMEM((4, 32), bf16),
        pltpu.SemaphoreType.DMA((6,)),
        pltpu.VMEM((chans, nx, ny, nz), bf16),
        pltpu.SemaphoreType.DMA((4,)),
        pltpu.VMEM((32, 864), bf16),
        pltpu.VMEM((32, 864), bf16),
        pltpu.VMEM((64, 864), bf16),
        pltpu.VMEM((32, 1728), bf16),
        *[pltpu.VMEM((96, 96 * count), bf16) for count in (3, 2, 2, 1, 1)],
        *[pltpu.VMEM((96, 192 * count), bf16) for count in (3, 2, 2, 1, 1)],
        pltpu.VMEM((96, 864), bf16),
        pltpu.VMEM((nx, 32 * ny, LANES), f32),
        pltpu.VMEM((nx, 96, (ny + 2) * LANES), f32),
        fine(96),
        coarse(96),
        coarse(16),
        coarse(32),
        fine(192),
        fine(96),
        fine(96),
        coarse(192),
        coarse(32),
        fine(96),
        pltpu.VMEM((nx, 32, ny * LANES), f32),
        pltpu.VMEM((cx, 64, cy * LANES), f32),
        pltpu.VMEM((nx, 96, ny * LANES), f32),
        pltpu.VMEM((4, 32), f32),
        pltpu.VMEM((96, 1024), f32),
        pltpu.VMEM((64, 1024), f32),
        pltpu.VMEM((96, 384), f32),
    ]
    scratch += [pltpu.VMEM((near, rows, length), bf16) for rows, length in pieces]
    scratch += [pltpu.VMEM((near, rows, length), bf16) for rows, length in pieces]
    scratch += [pltpu.VMEM((far, rows, length), bf16) for rows, length in pieces]
    scratch += [pltpu.VMEM((near, rows, length), bf16) for rows, length in pieces]
    scratch += [pltpu.SemaphoreType.DMA((7, 8))] * 2
    scratch += [pltpu.SemaphoreType.DMA((3,))] * 2
    scratch += [pltpu.SemaphoreType.DMA((3,))] * 2
    scratch += [pltpu.SemaphoreType.DMA((3,))] * 2

    vmem = pl.BlockSpec(memory_space=pltpu.VMEM)
    partial_outputs = pl.pallas_call(
        functools.partial(kernel, (nb, nsx, nsy, nx, ny)),
        out_shape=(
            jax.ShapeDtypeStruct((chans, nx, ny, nz), bf16),
            *[jax.ShapeDtypeStruct((near, rows, length), bf16) for rows, length in pieces],
        ),
        in_specs=[pl.BlockSpec(memory_space=pl.ANY)] * 6,
        out_specs=[pl.BlockSpec(memory_space=pl.ANY)] * 4,
        scratch_shapes=scratch,
        compiler_params=pltpu.CompilerParams(
            collective_id=0, has_side_effects=True, vmem_limit_bytes=62 * 1024 * 1024
        ),
        name="unet_step",
    )(
        features[0],
        labels[0],
        w_enc.reshape(27, 32, 32),
        w_mid.swapaxes(3, 4).reshape(27, 32, 64),
        w_dec.reshape(27, 32, 96),
        w_out,
    )
    feature_grad, grad_enc, grad_mid, grad_dec, grad_out = pl.pallas_call(
        functools.partial(outputs, scale),
        out_shape=(
            jax.ShapeDtypeStruct((chans, nx, ny, nz), bf16),
            jax.ShapeDtypeStruct((27, 32, 32), f32),
            jax.ShapeDtypeStruct((27, 32, 64), f32),
            jax.ShapeDtypeStruct((27, 32, 96), f32),
            jax.ShapeDtypeStruct((4, 32), f32),
        ),
        in_specs=[pl.BlockSpec(memory_space=pl.ANY)] * 4,
        out_specs=[pl.BlockSpec(memory_space=pl.ANY)] * 5,
        scratch_shapes=[
            pltpu.VMEM((chans, nx, ny, nz), bf16),
            *[pltpu.VMEM((near, rows, length), bf16) for rows, length in pieces],
            pltpu.VMEM((27, 32, 32), f32),
            pltpu.VMEM((27, 32, 64), f32),
            pltpu.VMEM((27, 32, 96), f32),
            pltpu.VMEM((4, 32), f32),
            pltpu.SemaphoreType.DMA((9,)),
        ],
        compiler_params=pltpu.CompilerParams(vmem_limit_bytes=62 * 1024 * 1024),
        name="unet_outputs",
    )(*partial_outputs)
    return (
        feature_grad[None],
        grad_enc.reshape(w_enc.shape),
        grad_mid.reshape(3, 3, 3, 32, 64).swapaxes(3, 4),
        grad_dec.reshape(w_dec.shape),
        grad_out,
    )


def solution(mesh):
    placed = (P("batch", None, "sx", "sy", None), P("batch", "sx", "sy", None), P(), P(), P(), P())
    return jax.shard_map(
        shards,
        mesh=mesh,
        in_specs=placed,
        out_specs=(P("batch", None, "sx", "sy", None), P(), P(), P(), P()),
        check_vma=False,
    )
```

profile of v0, /device:TPU:1, one launch (start us, length us, event | category | flops | bytes accessed | tf_op | source)
XLA Modules:
  0.0 59.4 jit_solution(17720369337467972624)
XLA Ops:
  0.6 56.5 %unet_step.1 = (bf16[32,4,8,128]{3,2,1,0:T(8,128)(2,1)}, bf16[8,96,128]{2,1,0:T(8,128)(2,1)}, bf16[8,64,128]{2,1,0:T(8,128)(2,1)}, bf16[8,48,128]{2,1,0:T(8,128)(2,1)}) custom-call(bf16[32,4,8,128]{3,2,1,0:T(8,128)(2,1)} %bitcast.13, s32[4,8,128]{2,1,0:T(8,128)} %bitcast.17, bf16[27,32,32]{2,1,0:T(8,128)(2,1)} %bitcast.14, bf16[27,32,64]{2,1,0:T(8,128)(2,1)} %bitcast.15, ...), custom_call_target="tpu_custom_call" | custom-call | tf_op jit(solution)/shard_map/unet_step/pallas_call | solution.py:947
  57.1 2.4 %unet_outputs.1 = (bf16[32,4,8,128]{3,2,1,0:T(8,128)(2,1)}, f32[27,32,32]{2,1,0:T(8,128)}, f32[27,32,64]{2,1,0:T(8,128)}, f32[27,32,96]{2,1,0:T(8,128)}, f32[4,32]{1,0:T(4,128)}) custom-call(bf16[32,4,8,128]{3,2,1,0:T(8,128)(2,1)} %get-tuple-element.14.features_in, bf16[8,96,128]{2,1,0:T(8,128)(2,1)} %get-tuple-element.15.dec_in, ...), custom_call_target="tpu_custom_call" | custom-call | tf_op jit(solution)/shard_map/unet_outputs/pallas_call | solution.py:968
where the time goes:
time: 59.6 us; the launch traced here: 59.4 us
  Pallas kernels  58.8 us (99%)
  between operations  0.64 us (1%)
    pallas_call x1, Pallas kernels, shards(): pl.pallas_call(functools.partial(kernel, (nb, nsx, nsy, nx, ny)), out_sha...  56.5 us
    pallas_call x1, Pallas kernels, shards(): pl.pallas_call(functools.partial(outputs, scale), out_shape=(jax.ShapeDty...  2.36 us

commit v1 on v0

--- a/solution.py
+++ b/solution.py
@@ -76,19 +76,20 @@
         step(at, carry)
 
 
-def over_halo(nx, ny, step):
+def over_halo(nx, ny, step, part=None):
     for x in range(nx + 2):
         for y in range(ny + 2):
-            if x in (0, nx + 1) or y in (0, ny + 1):
+            side = y in (0, ny + 1)
+            if (x in (0, nx + 1) or side) and (part is None or part != side):
                 step(x, y)
 
 
-def finish_halo(buf, nx, ny, chans, period, offset, shift, back=False):
+def finish_halo(buf, nx, ny, chans, period, offset, shift, back=False, part=None):
     def step(x, y):
         tile = buf[x, period + offset : period + offset + chans, lane_tile(y)].astype(f32)
         put_sides(buf, x, y, tile, period, offset, shift, back)
 
-    over_halo(nx, ny, step)
+    over_halo(nx, ny, step, part)
 
 
 def finish_inner(buf, nx, ny, chans, shift, back=False):
@@ -166,7 +167,7 @@
                 sums[x, :, lanes] += term
 
 
-def border_part(sums, weights, buf, nx, ny, first):
+def border_sides(sums, weights, buf, nx, ny, first):
     sides = (lane_tile(0), lane_tile(ny + 1))
     for x in range(nx):
         window = jnp.concatenate(
@@ -179,6 +180,9 @@
                 sums[x, :, lanes] = part
             else:
                 sums[x, :, lanes] += part
+
+
+def border_rows(sums, weights, buf, nx, ny):
     for x, a in ((0, 0), (nx - 1, 2)):
         for y in range(1, ny + 1, 2):
             lanes = lane_tile(y, 2)
@@ -434,8 +438,10 @@
             def _():
                 halo_copy(field, index).start()
 
-    def wait_halo(field):
+    def wait_halo(field, part=None):
         for index, (dx, dy) in enumerate(DIRS):
+            if part is not None and part != (dy == 0):
+                continue
 
             @pl.when(inside(-dx, -dy))
             def _():
@@ -561,21 +567,15 @@
     window_weights(skip_weights, w_dec, 64, 96)
     window_weights(up_weights, w_dec, 0, 64)
     out_total[...] = jnp.zeros(out_total.shape, f32)
-    wait_halo(FEAT)
-    finish_halo(F, nx, ny, 32, 32, 0, 1)
-
-    def enc_sides(x, carry):
+    wait_halo(FEAT, False)
+    finish_halo(F, nx, ny, 32, 32, 0, 1, part=False)
+    for x in range(1, nx - 1):
         enc_tiles(x, (0, ny - 1))
-        return carry
-
-    each(1, nx - 1, enc_sides, 0)
-
-    def enc_ends(i, carry):
+    wait_halo(FEAT, True)
+    finish_halo(F, nx, ny, 32, 32, 0, 1, part=True)
+    for x in (0, nx - 1):
         for tiles in all_pairs(ny):
-            enc_tiles(i * (nx - 1), tiles)
-        return carry
-
-    each(0, 2, enc_ends, 0)
+            enc_tiles(x, tiles)
 
     def pool_block(bx, carry):
         for by in range(cy):
@@ -634,14 +634,15 @@
     local_part(window_sums, up_weights, JU, nx, ny, False)
     wait_halo(SKIP)
     finish_halo(JE, nx, ny, 32, 32, 0, 1)
-    border_part(window_sums, skip_weights, JE, nx, ny, True)
-    wait_halo(MID)
-    for bx in range(cx + 2):
-        for by in range(cy + 2):
-            if bx in (0, cx + 1) or by in (0, cy + 1):
-                spread(bx, by, unpacked(UP[bx, :, lane_tile(by)]))
-
-    border_part(window_sums, up_weights, JU, nx, ny, False)
+    border_sides(window_sums, skip_weights, JE, nx, ny, True)
+    border_rows(window_sums, skip_weights, JE, nx, ny)
+    for part in (False, True):
+        wait_halo(MID, part)
+        over_halo(cx, cy, lambda bx, by: spread(bx, by, unpacked(UP[bx, :, lane_tile(by)])), part)
+        if part:
+            border_rows(window_sums, up_weights, JU, nx, ny)
+        else:
+            border_sides(window_sums, up_weights, JU, nx, ny, False)
 
     def dec_row(x, carry):
         pre = (
@@ -691,21 +692,15 @@
     total_dec[0:4, 864:896] = out_total[...]
     start_scatter(DEC)
 
-    wait_halo(DECG)
-    finish_halo(D, nx, ny, 32, 32, 0, 1, back=True)
-
-    def dec_back_sides(x, carry):
+    wait_halo(DECG, False)
+    finish_halo(D, nx, ny, 32, 32, 0, 1, back=True, part=False)
+    for x in range(1, nx - 1):
         dec_back(x, (0, ny - 1))
-        return carry
-
-    each(1, nx - 1, dec_back_sides, 0)
-
-    def dec_back_ends(i, carry):
+    wait_halo(DECG, True)
+    finish_halo(D, nx, ny, 32, 32, 0, 1, back=True, part=True)
+    for x in (0, nx - 1):
         for tiles in all_pairs(ny):
-            dec_back(i * (nx - 1), tiles)
-        return carry
-
-    each(0, 2, dec_back_ends, 0)
+            dec_back(x, tiles)
 
     def mid_grads(bx, carry):
         for by in range(cy):

time: 59.6 us -> 59.7 us (level)
  no operation moved by 1% of the time
where the time goes in v1:
time: 59.7 us; the launch traced here: 59.6 us
  Pallas kernels  58.9 us (99%)
  between operations  0.64 us (1%)
    pallas_call x1, Pallas kernels, shards(): pl.pallas_call(functools.partial(kernel, (nb, nsx, nsy, nx, ny)), out_sha...  56.6 us
    pallas_call x1, Pallas kernels, shards(): pl.pallas_call(functools.partial(outputs, scale), out_shape=(jax.ShapeDty...  2.36 us

profile of v1, /device:TPU:1, one launch (start us, length us, event | category | flops | bytes accessed | tf_op | source)
XLA Modules:
  0.0 59.6 jit_solution(10556875369257805344)
XLA Ops:
  0.6 56.6 %unet_step.1 = (bf16[32,4,8,128]{3,2,1,0:T(8,128)(2,1)}, bf16[8,96,128]{2,1,0:T(8,128)(2,1)}, bf16[8,64,128]{2,1,0:T(8,128)(2,1)}, bf16[8,48,128]{2,1,0:T(8,128)(2,1)}) custom-call(bf16[32,4,8,128]{3,2,1,0:T(8,128)(2,1)} %bitcast.13, s32[4,8,128]{2,1,0:T(8,128)} %bitcast.17, bf16[27,32,32]{2,1,0:T(8,128)(2,1)} %bitcast.14, bf16[27,32,64]{2,1,0:T(8,128)(2,1)} %bitcast.15, ...), custom_call_target="tpu_custom_call" | custom-call | tf_op jit(solution)/shard_map/unet_step/pallas_call | solution.py:942
  57.2 2.4 %unet_outputs.1 = (bf16[32,4,8,128]{3,2,1,0:T(8,128)(2,1)}, f32[27,32,32]{2,1,0:T(8,128)}, f32[27,32,64]{2,1,0:T(8,128)}, f32[27,32,96]{2,1,0:T(8,128)}, f32[4,32]{1,0:T(4,128)}) custom-call(bf16[32,4,8,128]{3,2,1,0:T(8,128)(2,1)} %get-tuple-element.14.features_in, bf16[8,96,128]{2,1,0:T(8,128)(2,1)} %get-tuple-element.15.dec_in, ...), custom_call_target="tpu_custom_call" | custom-call | tf_op jit(solution)/shard_map/unet_outputs/pallas_call | solution.py:963

commit v2 on v1

--- a/solution.py
+++ b/solution.py
@@ -739,10 +739,10 @@
         return carry
 
     each(0, cx, mid_back, 0)
-    start_halo(ENCG)
 
     weight_grad(total_enc, lambda x: EG[x + 1, :, lane_tile(1, ny)], [(F, 32, 32)], nx, ny)
     start_scatter(ENC)
+    start_halo(ENCG)
 
     def enc_back(x, tiles):
         grads = conv(w_enc_b, EG, x, tiles, back=True)

time: 59.7 us -> 59.6 us (level)
  no operation moved by 1% of the time
where the time goes in v2:
time: 59.6 us; the launch traced here: 59.4 us
  Pallas kernels  58.7 us (98%)
  between operations  0.64 us (1%)
    pallas_call x1, Pallas kernels, shards(): pl.pallas_call(functools.partial(kernel, (nb, nsx, nsy, nx, ny)), out_sha...  56.4 us
    pallas_call x1, Pallas kernels, shards(): pl.pallas_call(functools.partial(outputs, scale), out_shape=(jax.ShapeDty...  2.36 us

profile of v2, /device:TPU:1, one launch (start us, length us, event | category | flops | bytes accessed | tf_op | source)
XLA Modules:
  0.0 59.4 jit_solution(18092809149701556132)
XLA Ops:
  0.6 56.4 %unet_step.1 = (bf16[32,4,8,128]{3,2,1,0:T(8,128)(2,1)}, bf16[8,96,128]{2,1,0:T(8,128)(2,1)}, bf16[8,64,128]{2,1,0:T(8,128)(2,1)}, bf16[8,48,128]{2,1,0:T(8,128)(2,1)}) custom-call(bf16[32,4,8,128]{3,2,1,0:T(8,128)(2,1)} %bitcast.13, s32[4,8,128]{2,1,0:T(8,128)} %bitcast.17, bf16[27,32,32]{2,1,0:T(8,128)(2,1)} %bitcast.14, bf16[27,32,64]{2,1,0:T(8,128)(2,1)} %bitcast.15, ...), custom_call_target="tpu_custom_call" | custom-call | tf_op jit(solution)/shard_map/unet_step/pallas_call | solution.py:942
  57.0 2.4 %unet_outputs.1 = (bf16[32,4,8,128]{3,2,1,0:T(8,128)(2,1)}, f32[27,32,32]{2,1,0:T(8,128)}, f32[27,32,64]{2,1,0:T(8,128)}, f32[27,32,96]{2,1,0:T(8,128)}, f32[4,32]{1,0:T(4,128)}) custom-call(bf16[32,4,8,128]{3,2,1,0:T(8,128)(2,1)} %get-tuple-element.14.features_in, bf16[8,96,128]{2,1,0:T(8,128)(2,1)} %get-tuple-element.15.dec_in, ...), custom_call_target="tpu_custom_call" | custom-call | tf_op jit(solution)/shard_map/unet_outputs/pallas_call | solution.py:963
